TPU v7x, 256 devices: a whole 4x4x8 slice. The times are simulated.
256 devices in a mesh: pipe: 2 (over x_lo), ctx: 16 (over x_hi, z), tp: 8 (over y, core).
Axes of the slice: x: 4 (x_hi: 2, x_lo: 2; x = x_hi * 2 + x_lo), y: 4, z: 8, core: 2. Of those that a mesh axis runs over, the one named last changes fastest.
Arguments:
- fwd_queries: bfloat16 [2, 2048, 8192], P('pipe', 'ctx', 'tp'), may hold values from -6 to 6
- fwd_keyvals: bfloat16 [2, 2, 2048, 1024], P('pipe', None, 'ctx', 'tp'), may hold values from -6 to 6
- bwd_queries: bfloat16 [2, 2048, 8192], P('pipe', 'ctx', 'tp'), may hold values from -6 to 6
- bwd_keyvals: bfloat16 [2, 2, 2048, 1024], P('pipe', None, 'ctx', 'tp'), may hold values from -6 to 6
- bwd_cotangent: bfloat16 [2, 2048, 8192], P('pipe', 'ctx', 'tp'), may hold values from -6 to 6
- doc_lengths: int32 [2, 8], replicated, may hold values from 1 to 1024, 2048 in all within a row
- block_order: int32 [2, 16], replicated, may hold values from 0 to 15, each once within a row
Outputs:
- arrived_output: bfloat16 [2, 2048, 8192], P('pipe', 'ctx', 'tp')
- arrived_query_grad: bfloat16 [2, 2048, 8192], P('pipe', 'ctx', 'tp')
- arrived_keyval_grad: bfloat16 [2, 2, 2048, 1024], P('pipe', None, 'ctx', 'tp')
Inputs may be any that keep to these rules, and one draw needn't show every extreme that they name: `block_order`: each row is a permutation of 0 to 15. `doc_lengths`: each row sums to 2048.
All inputs are finite; a program needn't handle non-finite values.
Results may differ from a plain program's by a relative error of at most 0.023.
Values may be sent and summed in bfloat16 or wider, within the bound.
No kernel may reach another device: no remote copies, remote signals or barrier semaphores. Data moves between devices by JAX's collectives and lax.ppermute only.
A program may use at most 64 MiB of HBM per device.

v0:
```python
import jax
import jax.numpy as jnp
from jax import lax
from jax.experimental import pallas as pl
from jax.experimental.pallas import tpu as pltpu
from jax.sharding import PartitionSpec as P

HD = 128
BLOCK = 128
GROUP = 8
ROWS = GROUP * BLOCK
WIDE = 2 * BLOCK
SLOTS = 16
PAIRS = 2 * 8 + 2
BEYOND = 1 << 20
EXTRA = 16
FINAL = 128 + EXTRA
PACK = 12
HOLD = 0
ADD = 12
GRADS = 40
TURN = 12
FORWARD = 12
FINISH = 4
RING = 8
OFFSETS = (0, -3, 3, -1, -4, 2, 1, -2)
SCALE = HD**-0.5
LOG2E = 1.4426950408889634
NEG = -1e30


def prepare(batch, table, slots, sides, bases, first, place):
    me = lax.axis_index("ctx")
    half, z = me // RING, me % RING
    query_bases, leasts = [], []
    for side in range(2):
        owner = (half + side) % 2 * RING + z
        query_base = table[batch, owner] * BLOCK
        at = query_base + lax.broadcasted_iota(jnp.int32, (8, BLOCK), 1)
        start = jnp.zeros((8, BLOCK), jnp.int32)
        least = jnp.int32(0)
        end = jnp.int32(0)
        for i in range(SLOTS, table.shape[1]):
            end = end + table[batch, i]
            start = jnp.where(at >= end, end, start)
            least = jnp.where(query_base >= end, end, least)
        first[side] = start
        place[side] = at
        query_bases.append(query_base)
        leasts.append(least)
    count = jnp.int32(0)
    for side in range(2):
        for slot in range(RING):
            owner = half * RING + (z + (OFFSETS[slot] + RING)) % RING
            base = table[batch, owner] * BLOCK
            slots[count] = slot
            sides[count] = side
            bases[count] = base
            active = (base <= query_bases[side]) & (base + (BLOCK - 1) >= leasts[side])
            count = count + active.astype(jnp.int32)
        slots[count] = 0
        bases[count] = BEYOND
        count = count + count % 2
    return count // 2


def dot(a, b):
    return jnp.dot(a, b, preferred_element_type=jnp.float32)


def add(*terms):
    total = terms[0].astype(jnp.float32)
    for term in terms[1:]:
        total = total + term.astype(jnp.float32)
    return total.astype(jnp.bfloat16)


def turn(ref, flat, tall=None):
    for h in range(GROUP):
        part = ref[0, :, h * HD : (h + 1) * HD]
        flat[:, h * BLOCK : (h + 1) * BLOCK] = part.T
        if tall is not None:
            tall[h * BLOCK : (h + 1) * BLOCK, :] = part


def total_kernel(own, below, above, _, out):
    out[0] = add(own[...], below[...], above[...])


def turn_kernel(q, c, q_far, c_far, later, _, q_t, c_t, q_rows, c_rows, held):
    turn(later, held.at[0])
    turn(q, q_t.at[0], q_rows.at[0])
    turn(c, c_t.at[0], c_rows.at[0])
    turn(q_far, q_t.at[1], q_rows.at[1])
    turn(c_far, c_t.at[1], c_rows.at[1])


def allowed(i, side, bases, first, place):
    row = bases[i] + lax.broadcasted_iota(jnp.int32, (BLOCK, BLOCK), 0)
    return (row >= first[side, 0:1]) & (row <= place[side, 0:1])


def masked_scores(key, q_t, side, mask, c):
    s = dot(key, q_t[side, :, c * WIDE : (c + 1) * WIDE])
    return [
        jnp.where(mask, s[:, j * BLOCK : (j + 1) * BLOCK], NEG) for j in range(WIDE // BLOCK)
    ]


def fold(x, op):
    return op(x.reshape(x.shape[0] // 8, 8, x.shape[1]), axis=0)


def largest(count, slots, sides, bases, first, place, kv, q_t, scores, tops):
    def body(g, _):
        side = sides[2 * g]
        keys = [kv[slots[2 * g + j], 0] for j in range(2)]
        masks = [allowed(2 * g + j, side, bases, first, place) for j in range(2)]
        for c in range(ROWS // WIDE):
            for j in range(2):
                for k, part in enumerate(masked_scores(keys[j], q_t, side, masks[j], c)):
                    at = slice(c * WIDE + k * BLOCK, c * WIDE + (k + 1) * BLOCK)
                    scores[2 * g + j, :, at] = part
                    tops[side, :, at] = jnp.maximum(tops[side, :, at], fold(part, jnp.max))
        return 0

    lax.fori_loop(0, count, body, 0)
    for side in range(2):
        tops[side] = jnp.broadcast_to(jnp.max(tops[side], axis=0, keepdims=True), (8, ROWS))


def statistics(count, slots, sides, bases, first, place, kv, q_t, c_t, scores, tops, totals, deltas):
    tops[...] = jnp.full(tops.shape, NEG, jnp.float32)
    totals[...] = jnp.zeros(totals.shape, jnp.float32)
    deltas[...] = jnp.zeros(deltas.shape, jnp.float32)

    largest(count, slots, sides, bases, first, place, kv, q_t, scores, tops)

    def sums(g, _):
        side = sides[2 * g]
        values = [kv[slots[2 * g + j], 1] for j in range(2)]
        for c in range(ROWS // WIDE):
            at = slice(c * WIDE, (c + 1) * WIDE)
            for j in range(2):
                p = jnp.exp2((scores[2 * g + j, :, at] - tops[side, 0:1, at]) * (SCALE * LOG2E))
                totals[side, :, at] += fold(p, jnp.sum)
                deltas[side, :, at] += fold(p * dot(values[j], c_t[side, :, at]), jnp.sum)
        return 0

    lax.fori_loop(0, count, sums, 0)
    rows = []
    for side in range(2):
        rows.append(tops[side, 0:1])
        rows.append(jnp.sum(totals[side], axis=0, keepdims=True))
        rows.append(jnp.sum(deltas[side], axis=0, keepdims=True))
    rows.append(jnp.zeros((8 - len(rows), ROWS), jnp.float32))
    return jnp.concatenate(rows, axis=0)


def merge(mine, other, per_side=3):
    merged = []
    for side in range(2):
        a = [mine[side * per_side + r : side * per_side + r + 1, :] for r in range(per_side)]
        b = [other[(1 - side) * per_side + r : (1 - side) * per_side + r + 1, :] for r in range(per_side)]
        top = jnp.maximum(a[0], b[0])
        fa = jnp.exp2((a[0] - top) * (SCALE * LOG2E))
        fb = jnp.exp2((b[0] - top) * (SCALE * LOG2E))
        merged.append([top] + [x * fa + y * fb for x, y in zip(a[1:], b[1:])])
    return merged


def backward_stats_kernel(
    table, q_t, c_t, near, out,
    slots, sides, bases, first, place, scores, tops, totals, deltas,
):
    count = prepare(0, table, slots, sides, bases, first, place)
    out[...] = statistics(
        count, slots, sides, bases, first, place, near, q_t, c_t, scores, tops, totals, deltas
    )


def thirds(x):
    parts = []
    for _ in range(3):
        part = x.astype(jnp.bfloat16).astype(jnp.float32)
        parts.append(part)
        x = x - part
    return parts


def forward_kernel(
    table, q, q_far, near, dq, dq_far, out, out_far,
    slots, sides, bases, first, place, q_t, scores, tops, totals, acc, turned, probs,
):
    count = prepare(1, table, slots, sides, bases, first, place)
    q_t[0], q_t[1] = q[0], q_far[0]
    tops[...] = jnp.full(tops.shape, NEG, jnp.float32)
    totals[...] = jnp.zeros(totals.shape, jnp.float32)
    acc[...] = jnp.zeros_like(acc)
    largest(count, slots, sides, bases, first, place, near, q_t, scores, tops)

    def body(g, _):
        side = sides[2 * g]
        for j in range(2):
            turned[:, j * BLOCK : (j + 1) * BLOCK] = near[slots[2 * g + j], 1].T
        for c in range(ROWS // WIDE):
            at = slice(c * WIDE, (c + 1) * WIDE)
            for j in range(2):
                p = jnp.exp2((scores[2 * g + j, :, at] - tops[side, 0:1, at]) * (SCALE * LOG2E))
                totals[side, :, at] += fold(p, jnp.sum)
                probs[j * BLOCK : (j + 1) * BLOCK, at] = p.astype(jnp.bfloat16)
        acc[side] += dot(turned[...], probs[...])
        return 0

    lax.fori_loop(0, count, body, 0)
    for side, (ref, grad) in enumerate(((out, dq), (out_far, dq_far))):
        ref[0, FINAL:] = grad[0]
        total = jnp.sum(totals[side], axis=0, keepdims=True)
        total = jnp.maximum(total, 1e-30)
        ref[0, :HD] = (acc[side] * (1.0 / total)).astype(jnp.bfloat16)
        logs = tops[side, 0:1] * (SCALE * LOG2E) + jnp.log2(total)
        pad = jnp.zeros((EXTRA - 3, ROWS), jnp.float32)
        ref[0, HD:FINAL] = jnp.concatenate(thirds(logs) + [pad], axis=0).astype(jnp.bfloat16)


def add_kernel(keep, low, high, _, own, below, above):
    own[...] = add(keep[0], low[0], high[0])
    below[...] = add(keep[1], low[1], high[1])
    above[...] = add(keep[2], low[2])


def pack_kernel(x, below, above, three, two, three_later, two_later):
    for batch, (wide, narrow) in enumerate(((three, two), (three_later, two_later))):
        for i, ref in enumerate((x, below, above)):
            wide[i] = ref[batch, 0]
            if i < 2:
                narrow[i] = ref[batch, 0]


def hold_kernel(x, _, out):
    out[...] = x[...]


def finish_kernel(a, b, query_grad, output, token):
    token[...] = jnp.zeros(token.shape, token.dtype)
    logs = []
    for ref in (a, b):
        rows = ref[0, HD:FINAL].astype(jnp.float32)
        logs.append(rows[0:1] + rows[1:2] + rows[2:3])
    top = jnp.maximum(logs[0], logs[1])
    wa, wb = jnp.exp2(logs[0] - top), jnp.exp2(logs[1] - top)
    inverse = 1.0 / (wa + wb)
    wa, wb = wa * inverse, wb * inverse
    for h in range(GROUP):
        at = slice(h * BLOCK, (h + 1) * BLOCK)
        x, y = a[0, :HD, at].astype(jnp.float32), b[0, :HD, at].astype(jnp.float32)
        output[0, :, at] = (x * wa[:, at] + y * wb[:, at]).astype(jnp.bfloat16).T
        query_grad[0, :, at] = add(a[0, FINAL:, at], b[0, FINAL:, at]).T


def backward_kernel(
    table, q_t, c_t, q_rows, c_rows, near, mine, other, dq, dq_far, keep, low, high,
    slots, sides, bases, first, place, rows, acc, dkv, turned, probs, dscores,
):
    count = prepare(0, table, slots, sides, bases, first, place)
    for side, (top, total, weighted) in enumerate(merge(mine, other)):
        rows[side, 0:1] = top * (SCALE * LOG2E) + jnp.log2(total)
        rows[side, 1:2] = weighted / total
    acc[...] = jnp.zeros_like(acc)
    dkv[...] = jnp.zeros_like(dkv)

    def grads(g, _):
        side = sides[2 * g]
        for j in range(2):
            at_rows = slice(j * BLOCK, (j + 1) * BLOCK)
            key = near[slots[2 * g + j], 0]
            value = near[slots[2 * g + j], 1]
            mask = allowed(2 * g + j, side, bases, first, place)
            turned[:, at_rows] = key.T
            for c in range(ROWS // WIDE):
                at = slice(c * WIDE, (c + 1) * WIDE)
                s = jnp.concatenate(masked_scores(key, q_t, side, mask, c), axis=1)
                p = jnp.exp2(s * (SCALE * LOG2E) - rows[side, 0:1, at])
                dp = dot(value, c_t[side, :, at])
                probs[at_rows, at] = p.astype(jnp.bfloat16)
                dscores[at_rows, at] = (p * (dp - rows[side, 1:2, at])).astype(jnp.bfloat16)
        dv = dot(probs[...], c_rows[side])
        dk = dot(dscores[...], q_rows[side]) * SCALE
        acc[side] += dot(turned[...], dscores[...])
        for j in range(2):
            at_rows = slice(j * BLOCK, (j + 1) * BLOCK)
            dkv[slots[2 * g + j], 0] += dk[at_rows]
            dkv[slots[2 * g + j], 1] += dv[at_rows]
        return 0

    lax.fori_loop(0, count, grads, 0)
    keep[...] = dkv[0:3].astype(jnp.bfloat16)
    low[...] = dkv[3:6].astype(jnp.bfloat16)
    high[...] = dkv[6:8].astype(jnp.bfloat16)
    for side, ref in enumerate((dq, dq_far)):
        ref[0] = (acc[side] * SCALE).astype(jnp.bfloat16)


SMEM = pl.BlockSpec(memory_space=pltpu.SMEM)
VMEM = pl.BlockSpec(memory_space=pltpu.VMEM)
WHOLE = jax.ShapeDtypeStruct((1, BLOCK, GROUP * HD), jnp.bfloat16)
TOKEN = jax.ShapeDtypeStruct((8, 128), jnp.float32)
STATS = jax.ShapeDtypeStruct((8, ROWS), jnp.float32)
LIST = pltpu.SMEM((PAIRS + 1,), jnp.int32)
PLACES = pltpu.VMEM((2, 8, BLOCK), jnp.int32)
LISTS = [LIST, LIST, LIST, PLACES, PLACES]
TALLS = jax.ShapeDtypeStruct((2, ROWS, HD), jnp.bfloat16)
FLAT1 = jax.ShapeDtypeStruct((1, HD, ROWS), jnp.bfloat16)
FLATS = jax.ShapeDtypeStruct((2, HD, ROWS), jnp.bfloat16)
FLAT = pltpu.VMEM((2, HD, ROWS), jnp.bfloat16)
PART = jax.ShapeDtypeStruct((2, BLOCK, HD), jnp.bfloat16)
TALLER = jax.ShapeDtypeStruct((1, FINAL + BLOCK, GROUP * HD), jnp.bfloat16)
SCORES = pltpu.VMEM((PAIRS, BLOCK, ROWS), jnp.float32)
ACC = pltpu.VMEM((2, HD, ROWS), jnp.float32)
TURNED = pltpu.VMEM((HD, 2 * BLOCK), jnp.bfloat16)
PROBS = pltpu.VMEM((2 * BLOCK, ROWS), jnp.bfloat16)
SUMS = pltpu.VMEM((2, 8, ROWS), jnp.float32)
DKV = pltpu.VMEM((RING, 2, BLOCK, HD), jnp.float32)


def blocks(n):
    return jax.ShapeDtypeStruct((n, 2, BLOCK, HD), jnp.bfloat16)


def kernel(body, name, outs, scratch, cost, args, lists=()):
    single = not isinstance(outs, tuple)
    return pl.pallas_call(
        body,
        out_shape=outs,
        in_specs=[SMEM] * len(lists) + [VMEM] * len(args),
        out_specs=VMEM if single else (VMEM,) * len(outs),
        scratch_shapes=(LISTS if lists else []) + scratch,
        compiler_params=pltpu.CompilerParams(vmem_limit_bytes=32 << 20),
        cost_estimate=pl.CostEstimate(
            flops=cost << 29, bytes_accessed=2 << 20, transcendentals=1 << 21
        ),
        name=name,
    )(*lists, *args)


def along_z(x, distance):
    route = [(i, i // RING * RING + (i + distance) % RING) for i in range(SLOTS)]
    return lax.ppermute(x, "ctx", route)


def across_x(x):
    return lax.ppermute(x, "ctx", [(i, i ^ RING) for i in range(SLOTS)])


def other_section(x, flip=0, distance=0):
    route = [
        (p * SLOTS + i, (1 - p) * SLOTS + (i // RING * RING + (i + distance) % RING ^ flip))
        for p in range(2)
        for i in range(SLOTS)
    ]
    return lax.ppermute(x, ("pipe", "ctx"), route)


def hold(x, after):
    return kernel(hold_kernel, "hold", jax.ShapeDtypeStruct(x.shape, x.dtype), [], HOLD, (x, after))


def gather(x):
    below, above = along_z(x, 3), along_z(x, -3)
    three, two, three_later, two_later = kernel(
        pack_kernel, "pack", (blocks(3), blocks(2), blocks(3), blocks(2)), [], PACK, (x, below, above)
    )
    near = jnp.concatenate([three, along_z(three, 1), along_z(two, -1)])
    near_later = jnp.concatenate([three_later, along_z(three_later, 1), along_z(two_later, -1)])
    return near, near_later, three


def shards(fwd_queries, fwd_keyvals, bwd_queries, bwd_keyvals, bwd_cotangent, doc_lengths, block_order):
    lists = (jnp.concatenate([block_order, doc_lengths], axis=1),)
    near, near_later, three = gather(jnp.stack([bwd_keyvals, fwd_keyvals]))
    q_t, c_t, q_rows, c_rows, held = kernel(
        turn_kernel, "turn", (FLATS, FLATS, TALLS, TALLS, FLAT1), [], TURN,
        (bwd_queries, bwd_cotangent, across_x(bwd_queries), across_x(bwd_cotangent), fwd_queries, three),
    )
    mine = kernel(
        backward_stats_kernel, "backward_stats", STATS,
        [SCORES, SUMS, SUMS, SUMS], 2, (q_t, c_t, near), lists,
    )
    other = across_x(mine)
    dq, dq_far, keep, low, high = kernel(
        backward_kernel, "backward_grads", (FLAT1, FLAT1, blocks(3), blocks(3), blocks(2)),
        [SUMS, ACC, DKV, TURNED, PROBS, PROBS], GRADS, (q_t, c_t, q_rows, c_rows, near, mine, other), lists,
    )
    low, high = along_z(low, -1), along_z(high, 1)
    held = hold(held, mine)
    out, out_far = kernel(
        forward_kernel, "forward", (TALLER, TALLER),
        [FLAT, SCORES, SUMS, SUMS, ACC, TURNED, PROBS], FORWARD, (held, across_x(held), near_later, dq, dq_far), lists,
    )
    own, below, above = kernel(
        add_kernel, "add", (PART, PART, PART), [], ADD, (keep, low, high, out),
    )
    out, out_far = other_section(out), other_section(out_far, RING)
    own, below, above = other_section(own), other_section(below, 0, -3), other_section(above, 0, 3)
    query_grad, output, token = kernel(
        finish_kernel, "finish", (WHOLE, WHOLE, TOKEN), [], FINISH, (out, out_far)
    )
    keyval_grad = kernel(
        total_kernel, "total", blocks(1), [], 0, (own, below, above, token)
    )
    return output, query_grad, keyval_grad


def solution(mesh):
    placed = (
        P("pipe", "ctx", "tp"),
        P("pipe", None, "ctx", "tp"),
        P("pipe", "ctx", "tp"),
        P("pipe", None, "ctx", "tp"),
        P("pipe", "ctx", "tp"),
        P(),
        P(),
    )
    return jax.shard_map(
        shards,
        mesh=mesh,
        in_specs=placed,
        out_specs=(P("pipe", "ctx", "tp"), P("pipe", "ctx", "tp"), P("pipe", None, "ctx", "tp")),
        check_vma=False,
    )
```

profile of v0, /device:TPU:8, one launch (start us, length us, event | category | flops | bytes accessed | tf_op | source)
XLA Modules:
  0.0 60.5 jit_solution(7758279228508819717)
XLA Ops:
  0.7 0.9 %pad_maximum_fusion.1.x = bf16[2,1,2,128,128]{4,3,2,1,0:T(8,128)(2,1)S(1)} fusion(bf16[1,1,2,128,128]{4,3,2,1,0:T(8,128)(2,1)} %bitcast.2, bf16[1,1,2,128,128]{4,3,2,1,0:T(8,128)(2,1)} %bitcast.3), kind=kLoop, calls=%fused_computation.1 | loop fusion | flops 65536 | bytes 262144 | tf_op jit(solution)/shard_map/stack | solution.py:380
  1.6 4.7 %collective-permute-start.2 = (bf16[2,1,2,128,128]{4,3,2,1,0:T(8,128)(2,1)S(1)}, bf16[2,1,2,128,128]{4,3,2,1,0:T(8,128)(2,1)S(1)}, u32[]{:S(2)}, u32[]{:S(2)}) collective-permute-start(bf16[2,1,2,128,128]{4,3,2,1,0:T(8,128)(2,1)S(1)} %pad_maximum_fusion.1.x), channel_id=1, source_target_pairs={{0,24},{8,32},{16,40},{24,48},{32,56},{40,0},{48,8},{56,16},{64,88... | collective-permute-start | bytes 393224 | tf_op jit(solution)/shard_map/ppermute | solution.py:348
  6.3 2.2 %collective-permute-start.3 = (bf16[2,1,2,128,128]{4,3,2,1,0:T(8,128)(2,1)S(1)}, bf16[2,1,2,128,128]{4,3,2,1,0:T(8,128)(2,1)S(1)}, u32[]{:S(2)}, u32[]{:S(2)}) collective-permute-start(bf16[2,1,2,128,128]{4,3,2,1,0:T(8,128)(2,1)S(1)} %pad_maximum_fusion.1.x), channel_id=1, source_target_pairs={{0,40},{8,48},{16,56},{24,0},{32,8},{40,16},{48,24},{56,32},{64,10... | collective-permute-start | bytes 393224 | tf_op jit(solution)/shard_map/ppermute | solution.py:348
  8.5 0.0 copy-done
  8.5 3.0 %collective-permute-start = (bf16[1,128,1024]{2,1,0:T(8,128)(2,1)S(1)}, bf16[1,128,1024]{2,1,0:T(8,128)(2,1)S(1)}, u32[]{:S(2)}, u32[]{:S(2)}) collective-permute-start(bf16[1,128,1024]{2,1,0:T(8,128)(2,1)S(1)} %copy-done), channel_id=1, source_target_pairs={{0,64},{8,72},{16,80},{24,88},{32,96},{40,104},{48,112},{56,120},{... | collective-permute-start | bytes 786440 | tf_op jit(solution)/shard_map/ppermute | solution.py:352
  11.5 0.5 collective-permute-start.1
  12.0 0.1 pad_add_fusion.table
  12.1 4.6 %collective-permute-done.2.below = bf16[2,1,2,128,128]{4,3,2,1,0:T(8,128)(2,1)S(1)} collective-permute-done((bf16[2,1,2,128,128]{4,3,2,1,0:T(8,128)(2,1)S(1)}, bf16[2,1,2,128,128]{4,3,2,1,0:T(8,128)(2,1)S(1)}, u32[]{:S(2)}, u32[]{:S(2)}) %collective-permute-start.2) | collective-permute-done | bytes 131104 | tf_op jit(solution)/shard_map/ppermute | solution.py:348
  16.7 0.0 collective-permute-done.3.above
  16.8 0.1 pack.1
  16.8 0.0 copy-start.1
  16.8 4.6 %collective-permute-start.4 = (bf16[3,2,128,128]{3,2,1,0:T(8,128)(2,1)S(1)}, bf16[3,2,128,128]{3,2,1,0:T(8,128)(2,1)S(1)}, u32[]{:S(2)}, u32[]{:S(2)}) collective-permute-start(bf16[3,2,128,128]{3,2,1,0:T(8,128)(2,1)S(1)} %get-tuple-element.25._), channel_id=1, source_target_pairs={{0,8},{8,16},{16,24},{24,32},{32,40},{40,48},{48,56},{56,0},{64,72... | collective-permute-start | bytes 589832 | tf_op jit(solution)/shard_map/ppermute | solution.py:348
  21.5 0.0 collective-permute-start.5
  21.5 2.0 %collective-permute-start.7 = (bf16[3,2,128,128]{3,2,1,0:T(8,128)(2,1)S(1)}, bf16[3,2,128,128]{3,2,1,0:T(8,128)(2,1)S(1)}, u32[]{:S(2)}, u32[]{:S(2)}) collective-permute-start(bf16[3,2,128,128]{3,2,1,0:T(8,128)(2,1)S(1)} %get-tuple-element.30), channel_id=1, source_target_pairs={{0,8},{8,16},{16,24},{24,32},{32,40},{40,48},{48,56},{56,0},{64,72... | collective-permute-start | bytes 589832 | tf_op jit(solution)/shard_map/ppermute | solution.py:348
  23.5 0.0 collective-permute-done.q_far
  23.5 1.3 %collective-permute-start.8 = (bf16[2,2,128,128]{3,2,1,0:T(8,128)(2,1)S(1)}, bf16[2,2,128,128]{3,2,1,0:T(8,128)(2,1)S(1)}, u32[]{:S(2)}, u32[]{:S(2)}) collective-permute-start(bf16[2,2,128,128]{3,2,1,0:T(8,128)(2,1)S(1)} %get-tuple-element.31), channel_id=1, source_target_pairs={{0,56},{8,0},{16,8},{24,16},{32,24},{40,32},{48,40},{56,48},{64,12... | collective-permute-start | bytes 393224 | tf_op jit(solution)/shard_map/ppermute | solution.py:348
  24.8 0.0 collective-permute-done.1.c_far
  24.8 0.0 copy-done.1
  24.8 0.5 turn.1
  25.3 1.5 %collective-permute-done.4 = bf16[3,2,128,128]{3,2,1,0:T(8,128)(2,1)S(1)} collective-permute-done((bf16[3,2,128,128]{3,2,1,0:T(8,128)(2,1)S(1)}, bf16[3,2,128,128]{3,2,1,0:T(8,128)(2,1)S(1)}, u32[]{:S(2)}, u32[]{:S(2)}) %collective-permute-start.4) | collective-permute-done | bytes 196640 | tf_op jit(solution)/shard_map/ppermute | solution.py:348
  26.9 0.8 %collective-permute-done.5 = bf16[2,2,128,128]{3,2,1,0:T(8,128)(2,1)S(1)} collective-permute-done((bf16[2,2,128,128]{3,2,1,0:T(8,128)(2,1)S(1)}, bf16[2,2,128,128]{3,2,1,0:T(8,128)(2,1)S(1)}, u32[]{:S(2)}, u32[]{:S(2)}) %collective-permute-start.5) | collective-permute-done | bytes 131104 | tf_op jit(solution)/shard_map/ppermute | solution.py:348
  27.7 2.0 %backward_stats.1._.mine = f32[8,1024]{1,0:T(8,128)S(1)} custom-call(s32[2,24]{1,0:T(2,128)S(1)} %pad_add_fusion.table, bf16[2,128,1024]{2,1,0:T(8,128)(2,1)S(1)} %get-tuple-element.27.q_t, bf16[2,128,1024]{2,1,0:T(8,128)(2,1)S(1)} %get-tuple-element.28.c_t, bf16[8,2,128,128]{3,2,1,0:T(8,128)(2,1)S(1)} %constant_dynamic-update-slice_fusion.near), custom_call_target="tpu_custom_call" | custom-call | flops 1073741824 | bytes 2097152 | tf_op jit(solution)/shard_map/backward_stats/pallas_call | solution.py:332
  29.6 2.5 %collective-permute-start.9 = (f32[8,1024]{1,0:T(8,128)S(1)}, f32[8,1024]{1,0:T(8,128)S(1)}, u32[]{:S(2)}, u32[]{:S(2)}) collective-permute-start(f32[8,1024]{1,0:T(8,128)S(1)} %backward_stats.1._.mine), channel_id=1, source_target_pairs={{0,64},{8,72},{16,80},{24,88},{32,96},{40,104},{48,112},{56,120},{... | collective-permute-start | bytes 98312 | tf_op jit(solution)/shard_map/ppermute | solution.py:352
  32.2 1.2 %collective-permute-start.6 = (bf16[1,128,1024]{2,1,0:T(8,128)(2,1)S(1)}, bf16[1,128,1024]{2,1,0:T(8,128)(2,1)S(1)}, u32[]{:S(2)}, u32[]{:S(2)}) collective-permute-start(bf16[1,128,1024]{2,1,0:T(8,128)(2,1)S(1)} %hold.1.q), channel_id=1, source_target_pairs={{0,64},{8,72},{16,80},{24,88},{32,96},{40,104},{48,112},{56,120},{... | collective-permute-start | bytes 786440 | tf_op jit(solution)/shard_map/ppermute | solution.py:352
  33.4 0.0 collective-permute-done.8
  33.4 0.0 collective-permute-done.7
  33.4 0.1 pad_maximum_fusion.near
  33.4 2.1 %collective-permute-done.9.other = f32[8,1024]{1,0:T(8,128)S(1)} collective-permute-done((f32[8,1024]{1,0:T(8,128)S(1)}, f32[8,1024]{1,0:T(8,128)S(1)}, u32[]{:S(2)}, u32[]{:S(2)}) %collective-permute-start.9) | collective-permute-done | bytes 32800 | tf_op jit(solution)/shard_map/ppermute | solution.py:352
  35.6 2.4 %backward_grads.1 = (bf16[1,128,1024]{2,1,0:T(8,128)(2,1)S(1)}, bf16[1,128,1024]{2,1,0:T(8,128)(2,1)S(1)}, bf16[3,2,128,128]{3,2,1,0:T(8,128)(2,1)S(1)}, bf16[3,...) custom-call(s32[2,24]{1,0:T(2,128)S(1)} %pad_add_fusion.table, bf16[2,128,1024]{2,1,0:T(8,128)(2,1)S(1)} %get-tuple-element.27.q_t, ...), custom_call_target="tpu_custom_call" | custom-call | flops 21474836480 | bytes 2097152 | tf_op jit(solution)/shard_map/backward_grads/pallas_call | solution.py:332
  38.0 2.3 %collective-permute-start.12 = (bf16[3,2,128,128]{3,2,1,0:T(8,128)(2,1)S(1)}, bf16[3,2,128,128]{3,2,1,0:T(8,128)(2,1)S(1)}, u32[]{:S(2)}, u32[]{:S(2)}) collective-permute-start(bf16[3,2,128,128]{3,2,1,0:T(8,128)(2,1)S(1)} %get-tuple-element.41), channel_id=1, source_target_pairs={{0,56},{8,0},{16,8},{24,16},{32,24},{40,32},{48,40},{56,48},{64,12... | collective-permute-start | bytes 589832 | tf_op jit(solution)/shard_map/ppermute | solution.py:348
  40.2 0.9 %collective-permute-start.13 = (bf16[2,2,128,128]{3,2,1,0:T(8,128)(2,1)S(1)}, bf16[2,2,128,128]{3,2,1,0:T(8,128)(2,1)S(1)}, u32[]{:S(2)}, u32[]{:S(2)}) collective-permute-start(bf16[2,2,128,128]{3,2,1,0:T(8,128)(2,1)S(1)} %get-tuple-element.42), channel_id=1, source_target_pairs={{0,8},{8,16},{16,24},{24,32},{32,40},{40,48},{48,56},{56,0},{64,72... | collective-permute-start | bytes 393224 | tf_op jit(solution)/shard_map/ppermute | solution.py:348
  41.2 0.0 collective-permute-done.6.q_far
  41.2 2.8 %forward.1 = (bf16[1,272,1024]{2,1,0:T(8,128)(2,1)S(1)}, bf16[1,272,1024]{2,1,0:T(8,128)(2,1)S(1)}) custom-call(s32[2,24]{1,0:T(2,128)S(1)} %pad_add_fusion.table, bf16[1,128,1024]{2,1,0:T(8,128)(2,1)S(1)} %hold.1.q, bf16[1,128,1024]{2,1,0:T(8,128)(2,1)S(1)} %collective-permute-done.6.q_far, bf16[8,2,128,128]{3,2,1,0:T(8,128)(2,1)S(1)} %pad_maximum_fusion.near, ...), custom_call_target="tpu_custom_call" | custom-call | flops 6442450944 | bytes 2097152 | tf_op jit(solution)/shard_map/forward/pallas_call | solution.py:332
  44.0 1.8 %collective-permute-start.10 = (bf16[1,272,1024]{2,1,0:T(8,128)(2,1)S(1)}, bf16[1,272,1024]{2,1,0:T(8,128)(2,1)S(1)}, u32[]{:S(2)}, u32[]{:S(2)}) collective-permute-start(bf16[1,272,1024]{2,1,0:T(8,128)(2,1)S(1)} %get-tuple-element.36._), channel_id=1, source_target_pairs={{0,128},{8,136},{16,144},{24,152},{32,160},{40,168},{48,176},{56,1... | collective-permute-start | bytes 1671176 | tf_op jit(solution)/shard_map/ppermute | solution.py:361
  45.8 1.0 %collective-permute-start.11 = (bf16[1,272,1024]{2,1,0:T(8,128)(2,1)S(1)}, bf16[1,272,1024]{2,1,0:T(8,128)(2,1)S(1)}, u32[]{:S(2)}, u32[]{:S(2)}) collective-permute-start(bf16[1,272,1024]{2,1,0:T(8,128)(2,1)S(1)} %get-tuple-element.37), channel_id=1, source_target_pairs={{0,192},{8,200},{16,208},{24,216},{32,224},{40,232},{48,240},{56,2... | collective-permute-start | bytes 1671176 | tf_op jit(solution)/shard_map/ppermute | solution.py:361
  46.9 0.0 collective-permute-done.13.high
  46.9 0.0 collective-permute-done.12.low
  46.9 0.1 add.3
  46.9 1.1 %collective-permute-start.14 = (bf16[2,128,128]{2,1,0:T(8,128)(2,1)S(1)}, bf16[2,128,128]{2,1,0:T(8,128)(2,1)S(1)}, u32[]{:S(2)}, u32[]{:S(2)}) collective-permute-start(bf16[2,128,128]{2,1,0:T(8,128)(2,1)S(1)} %get-tuple-element.43), channel_id=1, source_target_pairs={{0,128},{8,136},{16,144},{24,152},{32,160},{40,168},{48,176},{56,1... | collective-permute-start | bytes 196616 | tf_op jit(solution)/shard_map/ppermute | solution.py:361
  48.1 3.5 %collective-permute-start.15 = (bf16[2,128,128]{2,1,0:T(8,128)(2,1)S(1)}, bf16[2,128,128]{2,1,0:T(8,128)(2,1)S(1)}, u32[]{:S(2)}, u32[]{:S(2)}) collective-permute-start(bf16[2,128,128]{2,1,0:T(8,128)(2,1)S(1)} %get-tuple-element.44), channel_id=1, source_target_pairs={{0,168},{8,176},{16,184},{24,128},{32,136},{40,144},{48,152},{56,1... | collective-permute-start | bytes 196616 | tf_op jit(solution)/shard_map/ppermute | solution.py:361
  51.5 2.0 %collective-permute-start.16 = (bf16[2,128,128]{2,1,0:T(8,128)(2,1)S(1)}, bf16[2,128,128]{2,1,0:T(8,128)(2,1)S(1)}, u32[]{:S(2)}, u32[]{:S(2)}) collective-permute-start(bf16[2,128,128]{2,1,0:T(8,128)(2,1)S(1)} %get-tuple-element.45), channel_id=1, source_target_pairs={{0,152},{8,160},{16,168},{24,176},{32,184},{40,128},{48,136},{56,1... | collective-permute-start | bytes 196616 | tf_op jit(solution)/shard_map/ppermute | solution.py:361
  53.6 3.3 %collective-permute-done.10.a = bf16[1,272,1024]{2,1,0:T(8,128)(2,1)S(1)} collective-permute-done((bf16[1,272,1024]{2,1,0:T(8,128)(2,1)S(1)}, bf16[1,272,1024]{2,1,0:T(8,128)(2,1)S(1)}, u32[]{:S(2)}, u32[]{:S(2)}) %collective-permute-start.10) | collective-permute-done | bytes 557088 | tf_op jit(solution)/shard_map/ppermute | solution.py:361
  56.9 0.0 collective-permute-done.11.b
  56.9 1.1 %finish.1 = (bf16[1,128,1024]{2,1,0:T(8,128)(2,1)}, bf16[1,128,1024]{2,1,0:T(8,128)(2,1)}, f32[8,128]{1,0:T(8,128)S(1)}) custom-call(bf16[1,272,1024]{2,1,0:T(8,128)(2,1)S(1)} %collective-permute-done.10.a, bf16[1,272,1024]{2,1,0:T(8,128)(2,1)S(1)} %collective-permute-done.11.b), custom_call_target="tpu_custom_call" | custom-call | flops 2147483648 | bytes 2097152 | tf_op jit(solution)/shard_map/finish/pallas_call | solution.py:332
  57.9 0.0 collective-permute-done.14.own
  58.0 0.0 collective-permute-done.15.below
  58.0 1.9 %collective-permute-done.16.above = bf16[2,128,128]{2,1,0:T(8,128)(2,1)S(1)} collective-permute-done((bf16[2,128,128]{2,1,0:T(8,128)(2,1)S(1)}, bf16[2,128,128]{2,1,0:T(8,128)(2,1)S(1)}, u32[]{:S(2)}, u32[]{:S(2)}) %collective-permute-start.16) | collective-permute-done | bytes 65568 | tf_op jit(solution)/shard_map/ppermute | solution.py:361
  59.8 0.7 %total.1 = bf16[1,2,128,128]{3,2,1,0:T(8,128)(2,1)} custom-call(bf16[2,128,128]{2,1,0:T(8,128)(2,1)S(1)} %collective-permute-done.14.own, bf16[2,128,128]{2,1,0:T(8,128)(2,1)S(1)} %collective-permute-done.15.below, bf16[2,128,128]{2,1,0:T(8,128)(2,1)S(1)} %collective-permute-done.16.above, f32[8,128]{1,0:T(8,128)S(1)} %get-tuple-element.46._), custom_call_target="tpu_custom_call" | custom-call | bytes 2097152 | tf_op jit(solution)/shard_map/total/pallas_call | solution.py:332
  (11 shorter events, 0.1 us)
Async XLA Ops:
  0.6 7.9 %copy-start = (bf16[1,128,1024]{2,1,0:T(8,128)(2,1)S(1)}, bf16[1,128,1024]{2,1,0:T(8,128)(2,1)}, u32[]{:S(2)}) copy-start(bf16[1,128,1024]{2,1,0:T(8,128)(2,1)} %q.1) | copy-start | bytes 786436
  0.6 11.4 %copy-start.3 = (s32[2,8]{1,0:T(2,128)S(1)}, s32[2,8]{1,0:T(2,128)}, u32[]{:S(2)}) copy-start(s32[2,8]{1,0:T(2,128)} %param.12) | copy-start | bytes 196
  0.7 11.4 %copy-start.4 = (s32[2,16]{1,0:T(2,128)S(1)}, s32[2,16]{1,0:T(2,128)}, u32[]{:S(2)}) copy-start(s32[2,16]{1,0:T(2,128)} %param.13) | copy-start | bytes 388
  1.6 15.2 %collective-permute-start.2 = (bf16[2,1,2,128,128]{4,3,2,1,0:T(8,128)(2,1)S(1)}, bf16[2,1,2,128,128]{4,3,2,1,0:T(8,128)(2,1)S(1)}, u32[]{:S(2)}, u32[]{:S(2)}) collective-permute-start(bf16[2,1,2,128,128]{4,3,2,1,0:T(8,128)(2,1)S(1)} %pad_maximum_fusion.1.x), channel_id=1, source_target_pairs={{0,24},{8,32},{16,40},{24,48},{32,56},{40,0},{48,8},{56,16},{64,88... | collective-permute-start | bytes 393224 | tf_op jit(solution)/shard_map/ppermute | solution.py:348
  6.3 10.5 %collective-permute-start.3 = (bf16[2,1,2,128,128]{4,3,2,1,0:T(8,128)(2,1)S(1)}, bf16[2,1,2,128,128]{4,3,2,1,0:T(8,128)(2,1)S(1)}, u32[]{:S(2)}, u32[]{:S(2)}) collective-permute-start(bf16[2,1,2,128,128]{4,3,2,1,0:T(8,128)(2,1)S(1)} %pad_maximum_fusion.1.x), channel_id=1, source_target_pairs={{0,40},{8,48},{16,56},{24,0},{32,8},{40,16},{48,24},{56,32},{64,10... | collective-permute-start | bytes 393224 | tf_op jit(solution)/shard_map/ppermute | solution.py:348
  8.5 15.0 %collective-permute-start = (bf16[1,128,1024]{2,1,0:T(8,128)(2,1)S(1)}, bf16[1,128,1024]{2,1,0:T(8,128)(2,1)S(1)}, u32[]{:S(2)}, u32[]{:S(2)}) collective-permute-start(bf16[1,128,1024]{2,1,0:T(8,128)(2,1)S(1)} %copy-done), channel_id=1, source_target_pairs={{0,64},{8,72},{16,80},{24,88},{32,96},{40,104},{48,112},{56,120},{... | collective-permute-start | bytes 786440 | tf_op jit(solution)/shard_map/ppermute | solution.py:352
  11.5 13.3 %collective-permute-start.1 = (bf16[1,128,1024]{2,1,0:T(8,128)(2,1)}, bf16[1,128,1024]{2,1,0:T(8,128)(2,1)S(1)}, u32[]{:S(2)}, u32[]{:S(2)}) collective-permute-start(bf16[1,128,1024]{2,1,0:T(8,128)(2,1)} %c.1), channel_id=1, source_target_pairs={{0,64},{8,72},{16,80},{24,88},{32,96},{40,104},{48,112},{56,120},{... | collective-permute-start | bytes 786440 | tf_op jit(solution)/shard_map/ppermute | solution.py:352
  16.7 8.1 %copy-start.2 = (bf16[1,128,1024]{2,1,0:T(8,128)(2,1)S(1)}, bf16[1,128,1024]{2,1,0:T(8,128)(2,1)}, u32[]{:S(2)}) copy-start(bf16[1,128,1024]{2,1,0:T(8,128)(2,1)} %later.1) | copy-start | bytes 786436
  16.8 8.0 %copy-start.1 = (bf16[1,128,1024]{2,1,0:T(8,128)(2,1)S(1)}, bf16[1,128,1024]{2,1,0:T(8,128)(2,1)}, u32[]{:S(2)}) copy-start(bf16[1,128,1024]{2,1,0:T(8,128)(2,1)} %c.1) | copy-start | bytes 786436
  16.8 10.0 %collective-permute-start.4 = (bf16[3,2,128,128]{3,2,1,0:T(8,128)(2,1)S(1)}, bf16[3,2,128,128]{3,2,1,0:T(8,128)(2,1)S(1)}, u32[]{:S(2)}, u32[]{:S(2)}) collective-permute-start(bf16[3,2,128,128]{3,2,1,0:T(8,128)(2,1)S(1)} %get-tuple-element.25._), channel_id=1, source_target_pairs={{0,8},{8,16},{16,24},{24,32},{32,40},{40,48},{48,56},{56,0},{64,72... | collective-permute-start | bytes 589832 | tf_op jit(solution)/shard_map/ppermute | solution.py:348
  21.5 6.2 %collective-permute-start.5 = (bf16[2,2,128,128]{3,2,1,0:T(8,128)(2,1)S(1)}, bf16[2,2,128,128]{3,2,1,0:T(8,128)(2,1)S(1)}, u32[]{:S(2)}, u32[]{:S(2)}) collective-permute-start(bf16[2,2,128,128]{3,2,1,0:T(8,128)(2,1)S(1)} %get-tuple-element.29), channel_id=1, source_target_pairs={{0,56},{8,0},{16,8},{24,16},{32,24},{40,32},{48,40},{56,48},{64,12... | collective-permute-start | bytes 393224 | tf_op jit(solution)/shard_map/ppermute | solution.py:348
  21.5 11.9 %collective-permute-start.7 = (bf16[3,2,128,128]{3,2,1,0:T(8,128)(2,1)S(1)}, bf16[3,2,128,128]{3,2,1,0:T(8,128)(2,1)S(1)}, u32[]{:S(2)}, u32[]{:S(2)}) collective-permute-start(bf16[3,2,128,128]{3,2,1,0:T(8,128)(2,1)S(1)} %get-tuple-element.30), channel_id=1, source_target_pairs={{0,8},{8,16},{16,24},{24,32},{32,40},{40,48},{48,56},{56,0},{64,72... | collective-permute-start | bytes 589832 | tf_op jit(solution)/shard_map/ppermute | solution.py:348
  23.5 9.8 %collective-permute-start.8 = (bf16[2,2,128,128]{3,2,1,0:T(8,128)(2,1)S(1)}, bf16[2,2,128,128]{3,2,1,0:T(8,128)(2,1)S(1)}, u32[]{:S(2)}, u32[]{:S(2)}) collective-permute-start(bf16[2,2,128,128]{3,2,1,0:T(8,128)(2,1)S(1)} %get-tuple-element.31), channel_id=1, source_target_pairs={{0,56},{8,0},{16,8},{24,16},{32,24},{40,32},{48,40},{56,48},{64,12... | collective-permute-start | bytes 393224 | tf_op jit(solution)/shard_map/ppermute | solution.py:348
  29.6 5.9 %collective-permute-start.9 = (f32[8,1024]{1,0:T(8,128)S(1)}, f32[8,1024]{1,0:T(8,128)S(1)}, u32[]{:S(2)}, u32[]{:S(2)}) collective-permute-start(f32[8,1024]{1,0:T(8,128)S(1)} %backward_stats.1._.mine), channel_id=1, source_target_pairs={{0,64},{8,72},{16,80},{24,88},{32,96},{40,104},{48,112},{56,120},{... | collective-permute-start | bytes 98312 | tf_op jit(solution)/shard_map/ppermute | solution.py:352
  32.2 9.0 %collective-permute-start.6 = (bf16[1,128,1024]{2,1,0:T(8,128)(2,1)S(1)}, bf16[1,128,1024]{2,1,0:T(8,128)(2,1)S(1)}, u32[]{:S(2)}, u32[]{:S(2)}) collective-permute-start(bf16[1,128,1024]{2,1,0:T(8,128)(2,1)S(1)} %hold.1.q), channel_id=1, source_target_pairs={{0,64},{8,72},{16,80},{24,88},{32,96},{40,104},{48,112},{56,120},{... | collective-permute-start | bytes 786440 | tf_op jit(solution)/shard_map/ppermute | solution.py:352
  38.0 8.9 %collective-permute-start.12 = (bf16[3,2,128,128]{3,2,1,0:T(8,128)(2,1)S(1)}, bf16[3,2,128,128]{3,2,1,0:T(8,128)(2,1)S(1)}, u32[]{:S(2)}, u32[]{:S(2)}) collective-permute-start(bf16[3,2,128,128]{3,2,1,0:T(8,128)(2,1)S(1)} %get-tuple-element.41), channel_id=1, source_target_pairs={{0,56},{8,0},{16,8},{24,16},{32,24},{40,32},{48,40},{56,48},{64,12... | collective-permute-start | bytes 589832 | tf_op jit(solution)/shard_map/ppermute | solution.py:348
  40.2 6.6 %collective-permute-start.13 = (bf16[2,2,128,128]{3,2,1,0:T(8,128)(2,1)S(1)}, bf16[2,2,128,128]{3,2,1,0:T(8,128)(2,1)S(1)}, u32[]{:S(2)}, u32[]{:S(2)}) collective-permute-start(bf16[2,2,128,128]{3,2,1,0:T(8,128)(2,1)S(1)} %get-tuple-element.42), channel_id=1, source_target_pairs={{0,8},{8,16},{16,24},{24,32},{32,40},{40,48},{48,56},{56,0},{64,72... | collective-permute-start | bytes 393224 | tf_op jit(solution)/shard_map/ppermute | solution.py:348
  44.0 12.9 %collective-permute-start.10 = (bf16[1,272,1024]{2,1,0:T(8,128)(2,1)S(1)}, bf16[1,272,1024]{2,1,0:T(8,128)(2,1)S(1)}, u32[]{:S(2)}, u32[]{:S(2)}) collective-permute-start(bf16[1,272,1024]{2,1,0:T(8,128)(2,1)S(1)} %get-tuple-element.36._), channel_id=1, source_target_pairs={{0,128},{8,136},{16,144},{24,152},{32,160},{40,168},{48,176},{56,1... | collective-permute-start | bytes 1671176 | tf_op jit(solution)/shard_map/ppermute | solution.py:361
  45.8 11.0 %collective-permute-start.11 = (bf16[1,272,1024]{2,1,0:T(8,128)(2,1)S(1)}, bf16[1,272,1024]{2,1,0:T(8,128)(2,1)S(1)}, u32[]{:S(2)}, u32[]{:S(2)}) collective-permute-start(bf16[1,272,1024]{2,1,0:T(8,128)(2,1)S(1)} %get-tuple-element.37), channel_id=1, source_target_pairs={{0,192},{8,200},{16,208},{24,216},{32,224},{40,232},{48,240},{56,2... | collective-permute-start | bytes 1671176 | tf_op jit(solution)/shard_map/ppermute | solution.py:361
  46.9 11.0 %collective-permute-start.14 = (bf16[2,128,128]{2,1,0:T(8,128)(2,1)S(1)}, bf16[2,128,128]{2,1,0:T(8,128)(2,1)S(1)}, u32[]{:S(2)}, u32[]{:S(2)}) collective-permute-start(bf16[2,128,128]{2,1,0:T(8,128)(2,1)S(1)} %get-tuple-element.43), channel_id=1, source_target_pairs={{0,128},{8,136},{16,144},{24,152},{32,160},{40,168},{48,176},{56,1... | collective-permute-start | bytes 196616 | tf_op jit(solution)/shard_map/ppermute | solution.py:361
  48.1 9.9 %collective-permute-start.15 = (bf16[2,128,128]{2,1,0:T(8,128)(2,1)S(1)}, bf16[2,128,128]{2,1,0:T(8,128)(2,1)S(1)}, u32[]{:S(2)}, u32[]{:S(2)}) collective-permute-start(bf16[2,128,128]{2,1,0:T(8,128)(2,1)S(1)} %get-tuple-element.44), channel_id=1, source_target_pairs={{0,168},{8,176},{16,184},{24,128},{32,136},{40,144},{48,152},{56,1... | collective-permute-start | bytes 196616 | tf_op jit(solution)/shard_map/ppermute | solution.py:361
  51.5 8.3 %collective-permute-start.16 = (bf16[2,128,128]{2,1,0:T(8,128)(2,1)S(1)}, bf16[2,128,128]{2,1,0:T(8,128)(2,1)S(1)}, u32[]{:S(2)}, u32[]{:S(2)}) collective-permute-start(bf16[2,128,128]{2,1,0:T(8,128)(2,1)S(1)} %get-tuple-element.45), channel_id=1, source_target_pairs={{0,152},{8,160},{16,168},{24,176},{32,184},{40,128},{48,136},{56,1... | collective-permute-start | bytes 196616 | tf_op jit(solution)/shard_map/ppermute | solution.py:361
where the time goes:
time: 61.2 us; the launch traced here: 60.5 us
  starting transfers between devices  34.8 us (57%)
  waiting for transfers between devices  14.2 us (23%)
  Pallas kernels  9.57 us (16%)
  other arithmetic  1.06 us (2%)
  between operations  0.75 us (1%)
    ppermute x8, starting transfers between devices, along_z(): return lax.ppermute(x, 'ctx', route)  18 us
    pallas_call x9, Pallas kernels, kernel(): pl.pallas_call(body, out_shape=outs, in_specs=[SMEM] * len(lists) + [VMEM...  9.57 us
    ppermute x5, starting transfers between devices, other_section(): return lax.ppermute(x, ('pipe', 'ctx'), route)  9.51 us
    ppermute x4, starting transfers between devices, across_x(): return lax.ppermute(x, 'ctx', [(i, i ^ RING) for i in range(SLOTS)])  7.23 us
    ppermute x8, waiting for transfers between devices, along_z(): return lax.ppermute(x, 'ctx', route)  6.96 us
    ppermute x5, waiting for transfers between devices, other_section(): return lax.ppermute(x, ('pipe', 'ctx'), route)  5.15 us
    ppermute x4, waiting for transfers between devices, across_x(): return lax.ppermute(x, 'ctx', [(i, i ^ RING) for i in range(SLOTS)])  2.13 us
  transfers between devices with their start and end apart: 17, of which 6 were waited for; matrix products, arithmetic and copies ran while one was open for 0% of the time, Pallas kernels for 15%

commit v1 on v0

--- a/solution.py
+++ b/solution.py
@@ -13,8 +13,8 @@
 SLOTS = 16
 PAIRS = 2 * 8 + 2
 BEYOND = 1 << 20
-EXTRA = 16
-FINAL = 128 + EXTRA
+EXTRA = 8
+FINAL = 2 * 128
 PACK = 12
 HOLD = 0
 ADD = 12
@@ -214,13 +214,13 @@
 
     lax.fori_loop(0, count, body, 0)
     for side, (ref, grad) in enumerate(((out, dq), (out_far, dq_far))):
-        ref[0, FINAL:] = grad[0]
+        ref[0, HD:FINAL] = grad[0]
         total = jnp.sum(totals[side], axis=0, keepdims=True)
         total = jnp.maximum(total, 1e-30)
         ref[0, :HD] = (acc[side] * (1.0 / total)).astype(jnp.bfloat16)
         logs = tops[side, 0:1] * (SCALE * LOG2E) + jnp.log2(total)
         pad = jnp.zeros((EXTRA - 3, ROWS), jnp.float32)
-        ref[0, HD:FINAL] = jnp.concatenate(thirds(logs) + [pad], axis=0).astype(jnp.bfloat16)
+        ref[0, FINAL:] = jnp.concatenate(thirds(logs) + [pad], axis=0).astype(jnp.bfloat16)
 
 
 def add_kernel(keep, low, high, _, own, below, above):
@@ -245,7 +245,7 @@
     token[...] = jnp.zeros(token.shape, token.dtype)
     logs = []
     for ref in (a, b):
-        rows = ref[0, HD:FINAL].astype(jnp.float32)
+        rows = ref[0, FINAL:].astype(jnp.float32)
         logs.append(rows[0:1] + rows[1:2] + rows[2:3])
     top = jnp.maximum(logs[0], logs[1])
     wa, wb = jnp.exp2(logs[0] - top), jnp.exp2(logs[1] - top)
@@ -255,7 +255,7 @@
         at = slice(h * BLOCK, (h + 1) * BLOCK)
         x, y = a[0, :HD, at].astype(jnp.float32), b[0, :HD, at].astype(jnp.float32)
         output[0, :, at] = (x * wa[:, at] + y * wb[:, at]).astype(jnp.bfloat16).T
-        query_grad[0, :, at] = add(a[0, FINAL:, at], b[0, FINAL:, at]).T
+        query_grad[0, :, at] = add(a[0, HD:FINAL, at], b[0, HD:FINAL, at]).T
 
 
 def backward_kernel(
@@ -314,7 +314,7 @@
 FLATS = jax.ShapeDtypeStruct((2, HD, ROWS), jnp.bfloat16)
 FLAT = pltpu.VMEM((2, HD, ROWS), jnp.bfloat16)
 PART = jax.ShapeDtypeStruct((2, BLOCK, HD), jnp.bfloat16)
-TALLER = jax.ShapeDtypeStruct((1, FINAL + BLOCK, GROUP * HD), jnp.bfloat16)
+TALLER = jax.ShapeDtypeStruct((1, FINAL + EXTRA, GROUP * HD), jnp.bfloat16)
 SCORES = pltpu.VMEM((PAIRS, BLOCK, ROWS), jnp.float32)
 ACC = pltpu.VMEM((2, HD, ROWS), jnp.float32)
 TURNED = pltpu.VMEM((HD, 2 * BLOCK), jnp.bfloat16)
@@ -401,7 +401,8 @@
         add_kernel, "add", (PART, PART, PART), [], ADD, (keep, low, high, out),
     )
     out, out_far = other_section(out), other_section(out_far, RING)
-    own, below, above = other_section(own), other_section(below, 0, -3), other_section(above, 0, 3)
+    below, above = other_section(below, 0, -3), other_section(above, 0, 3)
+    own = other_section(own)
     query_grad, output, token = kernel(
         finish_kernel, "finish", (WHOLE, WHOLE, TOKEN), [], FINISH, (out, out_far)
     )

time: 61.2 us -> 62.9 us (1.028)
  the two profiles are of different devices: /device:TPU:8 before, /device:TPU:40 now
where the time goes in v1:
time: 62.9 us; the launch traced here: 62.2 us
  starting transfers between devices  29 us (46%)
  waiting for transfers between devices  22.3 us (35%)
  Pallas kernels  8.92 us (14%)
  other arithmetic  1.06 us (2%)
  between operations  0.77 us (1%)
    ppermute x8, starting transfers between devices, along_z(): return lax.ppermute(x, 'ctx', route)  12.3 us
    ppermute x8, waiting for transfers between devices, along_z(): return lax.ppermute(x, 'ctx', route)  11.4 us
    ppermute x5, starting transfers between devices, other_section(): return lax.ppermute(x, ('pipe', 'ctx'), route)  9.5 us
    pallas_call x9, Pallas kernels, kernel(): pl.pallas_call(body, out_shape=outs, in_specs=[SMEM] * len(lists) + [VMEM...  8.92 us
    ppermute x5, waiting for transfers between devices, other_section(): return lax.ppermute(x, ('pipe', 'ctx'), route)  8.17 us
    ppermute x4, starting transfers between devices, across_x(): return lax.ppermute(x, 'ctx', [(i, i ^ RING) for i in range(SLOTS)])  7.23 us
    ppermute x4, waiting for transfers between devices, across_x(): return lax.ppermute(x, 'ctx', [(i, i ^ RING) for i in range(SLOTS)])  2.8 us
  transfers between devices with their start and end apart: 17, of which 7 were waited for; matrix products, arithmetic and copies ran while one was open for 0% of the time, Pallas kernels for 13%

profile of v1, /device:TPU:40, one launch (start us, length us, event | category | flops | bytes accessed | tf_op | source)
XLA Modules:
  0.0 62.2 jit_solution(17440586859616041087)
XLA Ops:
  0.6 0.0 copy-start
  0.6 0.0 copy-start.3
  0.7 0.9 %pad_maximum_fusion.1.x = bf16[2,1,2,128,128]{4,3,2,1,0:T(8,128)(2,1)S(1)} fusion(bf16[1,1,2,128,128]{4,3,2,1,0:T(8,128)(2,1)} %bitcast.2, bf16[1,1,2,128,128]{4,3,2,1,0:T(8,128)(2,1)} %bitcast.3), kind=kLoop, calls=%fused_computation.1 | loop fusion | flops 65536 | bytes 262144 | tf_op jit(solution)/shard_map/stack | solution.py:380
  1.6 5.9 %collective-permute-start.2 = (bf16[2,1,2,128,128]{4,3,2,1,0:T(8,128)(2,1)S(1)}, bf16[2,1,2,128,128]{4,3,2,1,0:T(8,128)(2,1)S(1)}, u32[]{:S(2)}, u32[]{:S(2)}) collective-permute-start(bf16[2,1,2,128,128]{4,3,2,1,0:T(8,128)(2,1)S(1)} %pad_maximum_fusion.1.x), channel_id=1, source_target_pairs={{0,24},{8,32},{16,40},{24,48},{32,56},{40,0},{48,8},{56,16},{64,88... | collective-permute-start | bytes 393224 | tf_op jit(solution)/shard_map/ppermute | solution.py:348
  7.5 0.1 collective-permute-start.3
  7.6 3.0 %collective-permute-start = (bf16[1,128,1024]{2,1,0:T(8,128)(2,1)S(1)}, bf16[1,128,1024]{2,1,0:T(8,128)(2,1)S(1)}, u32[]{:S(2)}, u32[]{:S(2)}) collective-permute-start(bf16[1,128,1024]{2,1,0:T(8,128)(2,1)S(1)} %copy-done), channel_id=1, source_target_pairs={{0,64},{8,72},{16,80},{24,88},{32,96},{40,104},{48,112},{56,120},{... | collective-permute-start | bytes 786440 | tf_op jit(solution)/shard_map/ppermute | solution.py:352
  10.6 0.5 collective-permute-start.1
  11.1 0.1 pad_add_fusion.table
  11.2 4.9 %collective-permute-done.2.below = bf16[2,1,2,128,128]{4,3,2,1,0:T(8,128)(2,1)S(1)} collective-permute-done((bf16[2,1,2,128,128]{4,3,2,1,0:T(8,128)(2,1)S(1)}, bf16[2,1,2,128,128]{4,3,2,1,0:T(8,128)(2,1)S(1)}, u32[]{:S(2)}, u32[]{:S(2)}) %collective-permute-start.2) | collective-permute-done | bytes 131104 | tf_op jit(solution)/shard_map/ppermute | solution.py:348
  16.2 3.2 %collective-permute-done.3.above = bf16[2,1,2,128,128]{4,3,2,1,0:T(8,128)(2,1)S(1)} collective-permute-done((bf16[2,1,2,128,128]{4,3,2,1,0:T(8,128)(2,1)S(1)}, bf16[2,1,2,128,128]{4,3,2,1,0:T(8,128)(2,1)S(1)}, u32[]{:S(2)}, u32[]{:S(2)}) %collective-permute-start.3) | collective-permute-done | bytes 131104 | tf_op jit(solution)/shard_map/ppermute | solution.py:348
  19.4 0.1 pack.1
  19.5 0.0 copy-start.1
  19.5 0.1 collective-permute-start.4
  19.6 2.0 %collective-permute-start.5 = (bf16[2,2,128,128]{3,2,1,0:T(8,128)(2,1)S(1)}, bf16[2,2,128,128]{3,2,1,0:T(8,128)(2,1)S(1)}, u32[]{:S(2)}, u32[]{:S(2)}) collective-permute-start(bf16[2,2,128,128]{3,2,1,0:T(8,128)(2,1)S(1)} %get-tuple-element.29), channel_id=1, source_target_pairs={{0,56},{8,0},{16,8},{24,16},{32,24},{40,32},{48,40},{56,48},{64,12... | collective-permute-start | bytes 393224 | tf_op jit(solution)/shard_map/ppermute | solution.py:348
  21.6 1.1 %collective-permute-start.7 = (bf16[3,2,128,128]{3,2,1,0:T(8,128)(2,1)S(1)}, bf16[3,2,128,128]{3,2,1,0:T(8,128)(2,1)S(1)}, u32[]{:S(2)}, u32[]{:S(2)}) collective-permute-start(bf16[3,2,128,128]{3,2,1,0:T(8,128)(2,1)S(1)} %get-tuple-element.30), channel_id=1, source_target_pairs={{0,8},{8,16},{16,24},{24,32},{32,40},{40,48},{48,56},{56,0},{64,72... | collective-permute-start | bytes 589832 | tf_op jit(solution)/shard_map/ppermute | solution.py:348
  22.7 0.0 collective-permute-done.q_far
  22.7 1.0 %collective-permute-start.8 = (bf16[2,2,128,128]{3,2,1,0:T(8,128)(2,1)S(1)}, bf16[2,2,128,128]{3,2,1,0:T(8,128)(2,1)S(1)}, u32[]{:S(2)}, u32[]{:S(2)}) collective-permute-start(bf16[2,2,128,128]{3,2,1,0:T(8,128)(2,1)S(1)} %get-tuple-element.31), channel_id=1, source_target_pairs={{0,56},{8,0},{16,8},{24,16},{32,24},{40,32},{48,40},{56,48},{64,12... | collective-permute-start | bytes 393224 | tf_op jit(solution)/shard_map/ppermute | solution.py:348
  23.7 0.0 collective-permute-done.1.c_far
  23.7 0.5 turn.1
  24.2 3.2 %collective-permute-done.4 = bf16[3,2,128,128]{3,2,1,0:T(8,128)(2,1)S(1)} collective-permute-done((bf16[3,2,128,128]{3,2,1,0:T(8,128)(2,1)S(1)}, bf16[3,2,128,128]{3,2,1,0:T(8,128)(2,1)S(1)}, u32[]{:S(2)}, u32[]{:S(2)}) %collective-permute-start.4) | collective-permute-done | bytes 196640 | tf_op jit(solution)/shard_map/ppermute | solution.py:348
  27.4 0.0 collective-permute-done.5
  27.5 2.0 %backward_stats.1._.mine = f32[8,1024]{1,0:T(8,128)S(1)} custom-call(s32[2,24]{1,0:T(2,128)S(1)} %pad_add_fusion.table, bf16[2,128,1024]{2,1,0:T(8,128)(2,1)S(1)} %get-tuple-element.27.q_t, bf16[2,128,1024]{2,1,0:T(8,128)(2,1)S(1)} %get-tuple-element.28.c_t, bf16[8,2,128,128]{3,2,1,0:T(8,128)(2,1)S(1)} %constant_dynamic-update-slice_fusion.near), custom_call_target="tpu_custom_call" | custom-call | flops 1073741824 | bytes 2097152 | tf_op jit(solution)/shard_map/backward_stats/pallas_call | solution.py:332
  29.4 3.1 %collective-permute-start.9 = (f32[8,1024]{1,0:T(8,128)S(1)}, f32[8,1024]{1,0:T(8,128)S(1)}, u32[]{:S(2)}, u32[]{:S(2)}) collective-permute-start(f32[8,1024]{1,0:T(8,128)S(1)} %backward_stats.1._.mine), channel_id=1, source_target_pairs={{0,64},{8,72},{16,80},{24,88},{32,96},{40,104},{48,112},{56,120},{... | collective-permute-start | bytes 98312 | tf_op jit(solution)/shard_map/ppermute | solution.py:352
  32.6 0.6 collective-permute-start.6
  33.1 0.0 collective-permute-done.8
  33.1 0.0 collective-permute-done.7
  33.1 0.1 pad_maximum_fusion.near
  33.2 2.1 %collective-permute-done.9.other = f32[8,1024]{1,0:T(8,128)S(1)} collective-permute-done((f32[8,1024]{1,0:T(8,128)S(1)}, f32[8,1024]{1,0:T(8,128)S(1)}, u32[]{:S(2)}, u32[]{:S(2)}) %collective-permute-start.9) | collective-permute-done | bytes 32800 | tf_op jit(solution)/shard_map/ppermute | solution.py:352
  35.3 2.4 %backward_grads.1 = (bf16[1,128,1024]{2,1,0:T(8,128)(2,1)S(1)}, bf16[1,128,1024]{2,1,0:T(8,128)(2,1)S(1)}, bf16[3,2,128,128]{3,2,1,0:T(8,128)(2,1)S(1)}, bf16[3,...) custom-call(s32[2,24]{1,0:T(2,128)S(1)} %pad_add_fusion.table, bf16[2,128,1024]{2,1,0:T(8,128)(2,1)S(1)} %get-tuple-element.27.q_t, ...), custom_call_target="tpu_custom_call" | custom-call | flops 21474836480 | bytes 2097152 | tf_op jit(solution)/shard_map/backward_grads/pallas_call | solution.py:332
  37.7 1.8 %collective-permute-start.12 = (bf16[3,2,128,128]{3,2,1,0:T(8,128)(2,1)S(1)}, bf16[3,2,128,128]{3,2,1,0:T(8,128)(2,1)S(1)}, u32[]{:S(2)}, u32[]{:S(2)}) collective-permute-start(bf16[3,2,128,128]{3,2,1,0:T(8,128)(2,1)S(1)} %get-tuple-element.41), channel_id=1, source_target_pairs={{0,56},{8,0},{16,8},{24,16},{32,24},{40,32},{48,40},{56,48},{64,12... | collective-permute-start | bytes 589832 | tf_op jit(solution)/shard_map/ppermute | solution.py:348
  39.5 0.3 collective-permute-start.13
  39.8 0.7 %collective-permute-done.6.q_far = bf16[1,128,1024]{2,1,0:T(8,128)(2,1)S(1)} collective-permute-done((bf16[1,128,1024]{2,1,0:T(8,128)(2,1)S(1)}, bf16[1,128,1024]{2,1,0:T(8,128)(2,1)S(1)}, u32[]{:S(2)}, u32[]{:S(2)}) %collective-permute-start.6) | collective-permute-done | bytes 262176 | tf_op jit(solution)/shard_map/ppermute | solution.py:352
  40.5 2.2 %forward.1 = (bf16[1,264,1024]{2,1,0:T(8,128)(2,1)S(1)}, bf16[1,264,1024]{2,1,0:T(8,128)(2,1)S(1)}) custom-call(s32[2,24]{1,0:T(2,128)S(1)} %pad_add_fusion.table, bf16[1,128,1024]{2,1,0:T(8,128)(2,1)S(1)} %hold.1.q, bf16[1,128,1024]{2,1,0:T(8,128)(2,1)S(1)} %collective-permute-done.6.q_far, bf16[8,2,128,128]{3,2,1,0:T(8,128)(2,1)S(1)} %pad_maximum_fusion.near, ...), custom_call_target="tpu_custom_call" | custom-call | flops 6442450944 | bytes 2097152 | tf_op jit(solution)/shard_map/forward/pallas_call | solution.py:332
  42.7 1.1 %collective-permute-start.10 = (bf16[1,264,1024]{2,1,0:T(8,128)(2,1)S(1)}, bf16[1,264,1024]{2,1,0:T(8,128)(2,1)S(1)}, u32[]{:S(2)}, u32[]{:S(2)}) collective-permute-start(bf16[1,264,1024]{2,1,0:T(8,128)(2,1)S(1)} %get-tuple-element.36._), channel_id=1, source_target_pairs={{0,128},{8,136},{16,144},{24,152},{32,160},{40,168},{48,176},{56,1... | collective-permute-start | bytes 1622024 | tf_op jit(solution)/shard_map/ppermute | solution.py:361
  43.8 1.0 %collective-permute-start.11 = (bf16[1,264,1024]{2,1,0:T(8,128)(2,1)S(1)}, bf16[1,264,1024]{2,1,0:T(8,128)(2,1)S(1)}, u32[]{:S(2)}, u32[]{:S(2)}) collective-permute-start(bf16[1,264,1024]{2,1,0:T(8,128)(2,1)S(1)} %get-tuple-element.37), channel_id=1, source_target_pairs={{0,192},{8,200},{16,208},{24,216},{32,224},{40,232},{48,240},{56,2... | collective-permute-start | bytes 1622024 | tf_op jit(solution)/shard_map/ppermute | solution.py:361
  44.8 0.0 collective-permute-done.13.high
  44.8 0.0 collective-permute-done.12.low
  44.8 0.1 add.3
  44.9 1.3 %collective-permute-start.14 = (bf16[2,128,128]{2,1,0:T(8,128)(2,1)S(1)}, bf16[2,128,128]{2,1,0:T(8,128)(2,1)S(1)}, u32[]{:S(2)}, u32[]{:S(2)}) collective-permute-start(bf16[2,128,128]{2,1,0:T(8,128)(2,1)S(1)} %get-tuple-element.43), channel_id=1, source_target_pairs={{0,128},{8,136},{16,144},{24,152},{32,160},{40,168},{48,176},{56,1... | collective-permute-start | bytes 196616 | tf_op jit(solution)/shard_map/ppermute | solution.py:361
  46.2 5.8 %collective-permute-start.15 = (bf16[2,128,128]{2,1,0:T(8,128)(2,1)S(1)}, bf16[2,128,128]{2,1,0:T(8,128)(2,1)S(1)}, u32[]{:S(2)}, u32[]{:S(2)}) collective-permute-start(bf16[2,128,128]{2,1,0:T(8,128)(2,1)S(1)} %get-tuple-element.44), channel_id=1, source_target_pairs={{0,168},{8,176},{16,184},{24,128},{32,136},{40,144},{48,152},{56,1... | collective-permute-start | bytes 196616 | tf_op jit(solution)/shard_map/ppermute | solution.py:361
  52.0 0.3 collective-permute-start.16
  52.3 3.6 %collective-permute-done.10.a = bf16[1,264,1024]{2,1,0:T(8,128)(2,1)S(1)} collective-permute-done((bf16[1,264,1024]{2,1,0:T(8,128)(2,1)S(1)}, bf16[1,264,1024]{2,1,0:T(8,128)(2,1)S(1)}, u32[]{:S(2)}, u32[]{:S(2)}) %collective-permute-start.10) | collective-permute-done | bytes 540704 | tf_op jit(solution)/shard_map/ppermute | solution.py:361
  55.9 0.0 collective-permute-done.11.b
  55.9 1.1 %finish.1 = (bf16[1,128,1024]{2,1,0:T(8,128)(2,1)}, bf16[1,128,1024]{2,1,0:T(8,128)(2,1)}, f32[8,128]{1,0:T(8,128)S(1)}) custom-call(bf16[1,264,1024]{2,1,0:T(8,128)(2,1)S(1)} %collective-permute-done.10.a, bf16[1,264,1024]{2,1,0:T(8,128)(2,1)S(1)} %collective-permute-done.11.b), custom_call_target="tpu_custom_call" | custom-call | flops 2147483648 | bytes 2097152 | tf_op jit(solution)/shard_map/finish/pallas_call | solution.py:332
  57.0 0.0 collective-permute-done.14.own
  57.0 0.0 collective-permute-done.15.below
  57.0 4.5 %collective-permute-done.16.above = bf16[2,128,128]{2,1,0:T(8,128)(2,1)S(1)} collective-permute-done((bf16[2,128,128]{2,1,0:T(8,128)(2,1)S(1)}, bf16[2,128,128]{2,1,0:T(8,128)(2,1)S(1)}, u32[]{:S(2)}, u32[]{:S(2)}) %collective-permute-start.16) | collective-permute-done | bytes 65568 | tf_op jit(solution)/shard_map/ppermute | solution.py:361
  61.5 0.7 %total.1 = bf16[1,2,128,128]{3,2,1,0:T(8,128)(2,1)} custom-call(bf16[2,128,128]{2,1,0:T(8,128)(2,1)S(1)} %collective-permute-done.14.own, bf16[2,128,128]{2,1,0:T(8,128)(2,1)S(1)} %collective-permute-done.15.below, bf16[2,128,128]{2,1,0:T(8,128)(2,1)S(1)} %collective-permute-done.16.above, f32[8,128]{1,0:T(8,128)S(1)} %get-tuple-element.46._), custom_call_target="tpu_custom_call" | custom-call | bytes 2097152 | tf_op jit(solution)/shard_map/total/pallas_call | solution.py:332
  (11 shorter events, 0.1 us)
Async XLA Ops:
  0.6 7.0 %copy-start = (bf16[1,128,1024]{2,1,0:T(8,128)(2,1)S(1)}, bf16[1,128,1024]{2,1,0:T(8,128)(2,1)}, u32[]{:S(2)}) copy-start(bf16[1,128,1024]{2,1,0:T(8,128)(2,1)} %q.1) | copy-start | bytes 786436
  0.6 10.5 %copy-start.3 = (s32[2,8]{1,0:T(2,128)S(1)}, s32[2,8]{1,0:T(2,128)}, u32[]{:S(2)}) copy-start(s32[2,8]{1,0:T(2,128)} %param.12) | copy-start | bytes 196
  0.7 10.5 %copy-start.4 = (s32[2,16]{1,0:T(2,128)S(1)}, s32[2,16]{1,0:T(2,128)}, u32[]{:S(2)}) copy-start(s32[2,16]{1,0:T(2,128)} %param.13) | copy-start | bytes 388
  1.6 14.6 %collective-permute-start.2 = (bf16[2,1,2,128,128]{4,3,2,1,0:T(8,128)(2,1)S(1)}, bf16[2,1,2,128,128]{4,3,2,1,0:T(8,128)(2,1)S(1)}, u32[]{:S(2)}, u32[]{:S(2)}) collective-permute-start(bf16[2,1,2,128,128]{4,3,2,1,0:T(8,128)(2,1)S(1)} %pad_maximum_fusion.1.x), channel_id=1, source_target_pairs={{0,24},{8,32},{16,40},{24,48},{32,56},{40,0},{48,8},{56,16},{64,88... | collective-permute-start | bytes 393224 | tf_op jit(solution)/shard_map/ppermute | solution.py:348
  7.5 11.9 %collective-permute-start.3 = (bf16[2,1,2,128,128]{4,3,2,1,0:T(8,128)(2,1)S(1)}, bf16[2,1,2,128,128]{4,3,2,1,0:T(8,128)(2,1)S(1)}, u32[]{:S(2)}, u32[]{:S(2)}) collective-permute-start(bf16[2,1,2,128,128]{4,3,2,1,0:T(8,128)(2,1)S(1)} %pad_maximum_fusion.1.x), channel_id=1, source_target_pairs={{0,40},{8,48},{16,56},{24,0},{32,8},{40,16},{48,24},{56,32},{64,10... | collective-permute-start | bytes 393224 | tf_op jit(solution)/shard_map/ppermute | solution.py:348
  7.6 15.0 %collective-permute-start = (bf16[1,128,1024]{2,1,0:T(8,128)(2,1)S(1)}, bf16[1,128,1024]{2,1,0:T(8,128)(2,1)S(1)}, u32[]{:S(2)}, u32[]{:S(2)}) collective-permute-start(bf16[1,128,1024]{2,1,0:T(8,128)(2,1)S(1)} %copy-done), channel_id=1, source_target_pairs={{0,64},{8,72},{16,80},{24,88},{32,96},{40,104},{48,112},{56,120},{... | collective-permute-start | bytes 786440 | tf_op jit(solution)/shard_map/ppermute | solution.py:352
  10.6 13.1 %collective-permute-start.1 = (bf16[1,128,1024]{2,1,0:T(8,128)(2,1)}, bf16[1,128,1024]{2,1,0:T(8,128)(2,1)S(1)}, u32[]{:S(2)}, u32[]{:S(2)}) collective-permute-start(bf16[1,128,1024]{2,1,0:T(8,128)(2,1)} %c.1), channel_id=1, source_target_pairs={{0,64},{8,72},{16,80},{24,88},{32,96},{40,104},{48,112},{56,120},{... | collective-permute-start | bytes 786440 | tf_op jit(solution)/shard_map/ppermute | solution.py:352
  19.4 4.3 %copy-start.2 = (bf16[1,128,1024]{2,1,0:T(8,128)(2,1)S(1)}, bf16[1,128,1024]{2,1,0:T(8,128)(2,1)}, u32[]{:S(2)}) copy-start(bf16[1,128,1024]{2,1,0:T(8,128)(2,1)} %later.1) | copy-start | bytes 786436
  19.5 4.3 %copy-start.1 = (bf16[1,128,1024]{2,1,0:T(8,128)(2,1)S(1)}, bf16[1,128,1024]{2,1,0:T(8,128)(2,1)}, u32[]{:S(2)}) copy-start(bf16[1,128,1024]{2,1,0:T(8,128)(2,1)} %c.1) | copy-start | bytes 786436
  19.5 7.9 %collective-permute-start.4 = (bf16[3,2,128,128]{3,2,1,0:T(8,128)(2,1)S(1)}, bf16[3,2,128,128]{3,2,1,0:T(8,128)(2,1)S(1)}, u32[]{:S(2)}, u32[]{:S(2)}) collective-permute-start(bf16[3,2,128,128]{3,2,1,0:T(8,128)(2,1)S(1)} %get-tuple-element.25._), channel_id=1, source_target_pairs={{0,8},{8,16},{16,24},{24,32},{32,40},{40,48},{48,56},{56,0},{64,72... | collective-permute-start | bytes 589832 | tf_op jit(solution)/shard_map/ppermute | solution.py:348
  19.6 7.9 %collective-permute-start.5 = (bf16[2,2,128,128]{3,2,1,0:T(8,128)(2,1)S(1)}, bf16[2,2,128,128]{3,2,1,0:T(8,128)(2,1)S(1)}, u32[]{:S(2)}, u32[]{:S(2)}) collective-permute-start(bf16[2,2,128,128]{3,2,1,0:T(8,128)(2,1)S(1)} %get-tuple-element.29), channel_id=1, source_target_pairs={{0,56},{8,0},{16,8},{24,16},{32,24},{40,32},{48,40},{56,48},{64,12... | collective-permute-start | bytes 393224 | tf_op jit(solution)/shard_map/ppermute | solution.py:348
  21.6 11.6 %collective-permute-start.7 = (bf16[3,2,128,128]{3,2,1,0:T(8,128)(2,1)S(1)}, bf16[3,2,128,128]{3,2,1,0:T(8,128)(2,1)S(1)}, u32[]{:S(2)}, u32[]{:S(2)}) collective-permute-start(bf16[3,2,128,128]{3,2,1,0:T(8,128)(2,1)S(1)} %get-tuple-element.30), channel_id=1, source_target_pairs={{0,8},{8,16},{16,24},{24,32},{32,40},{40,48},{48,56},{56,0},{64,72... | collective-permute-start | bytes 589832 | tf_op jit(solution)/shard_map/ppermute | solution.py:348
  22.7 10.5 %collective-permute-start.8 = (bf16[2,2,128,128]{3,2,1,0:T(8,128)(2,1)S(1)}, bf16[2,2,128,128]{3,2,1,0:T(8,128)(2,1)S(1)}, u32[]{:S(2)}, u32[]{:S(2)}) collective-permute-start(bf16[2,2,128,128]{3,2,1,0:T(8,128)(2,1)S(1)} %get-tuple-element.31), channel_id=1, source_target_pairs={{0,56},{8,0},{16,8},{24,16},{32,24},{40,32},{48,40},{56,48},{64,12... | collective-permute-start | bytes 393224 | tf_op jit(solution)/shard_map/ppermute | solution.py:348
  29.4 5.9 %collective-permute-start.9 = (f32[8,1024]{1,0:T(8,128)S(1)}, f32[8,1024]{1,0:T(8,128)S(1)}, u32[]{:S(2)}, u32[]{:S(2)}) collective-permute-start(f32[8,1024]{1,0:T(8,128)S(1)} %backward_stats.1._.mine), channel_id=1, source_target_pairs={{0,64},{8,72},{16,80},{24,88},{32,96},{40,104},{48,112},{56,120},{... | collective-permute-start | bytes 98312 | tf_op jit(solution)/shard_map/ppermute | solution.py:352
  32.6 8.0 %collective-permute-start.6 = (bf16[1,128,1024]{2,1,0:T(8,128)(2,1)S(1)}, bf16[1,128,1024]{2,1,0:T(8,128)(2,1)S(1)}, u32[]{:S(2)}, u32[]{:S(2)}) collective-permute-start(bf16[1,128,1024]{2,1,0:T(8,128)(2,1)S(1)} %hold.1.q), channel_id=1, source_target_pairs={{0,64},{8,72},{16,80},{24,88},{32,96},{40,104},{48,112},{56,120},{... | collective-permute-start | bytes 786440 | tf_op jit(solution)/shard_map/ppermute | solution.py:352
  37.7 7.2 %collective-permute-start.12 = (bf16[3,2,128,128]{3,2,1,0:T(8,128)(2,1)S(1)}, bf16[3,2,128,128]{3,2,1,0:T(8,128)(2,1)S(1)}, u32[]{:S(2)}, u32[]{:S(2)}) collective-permute-start(bf16[3,2,128,128]{3,2,1,0:T(8,128)(2,1)S(1)} %get-tuple-element.41), channel_id=1, source_target_pairs={{0,56},{8,0},{16,8},{24,16},{32,24},{40,32},{48,40},{56,48},{64,12... | collective-permute-start | bytes 589832 | tf_op jit(solution)/shard_map/ppermute | solution.py:348
  39.5 5.3 %collective-permute-start.13 = (bf16[2,2,128,128]{3,2,1,0:T(8,128)(2,1)S(1)}, bf16[2,2,128,128]{3,2,1,0:T(8,128)(2,1)S(1)}, u32[]{:S(2)}, u32[]{:S(2)}) collective-permute-start(bf16[2,2,128,128]{3,2,1,0:T(8,128)(2,1)S(1)} %get-tuple-element.42), channel_id=1, source_target_pairs={{0,8},{8,16},{16,24},{24,32},{32,40},{40,48},{48,56},{56,0},{64,72... | collective-permute-start | bytes 393224 | tf_op jit(solution)/shard_map/ppermute | solution.py:348
  42.7 13.2 %collective-permute-start.10 = (bf16[1,264,1024]{2,1,0:T(8,128)(2,1)S(1)}, bf16[1,264,1024]{2,1,0:T(8,128)(2,1)S(1)}, u32[]{:S(2)}, u32[]{:S(2)}) collective-permute-start(bf16[1,264,1024]{2,1,0:T(8,128)(2,1)S(1)} %get-tuple-element.36._), channel_id=1, source_target_pairs={{0,128},{8,136},{16,144},{24,152},{32,160},{40,168},{48,176},{56,1... | collective-permute-start | bytes 1622024 | tf_op jit(solution)/shard_map/ppermute | solution.py:361
  43.8 12.1 %collective-permute-start.11 = (bf16[1,264,1024]{2,1,0:T(8,128)(2,1)S(1)}, bf16[1,264,1024]{2,1,0:T(8,128)(2,1)S(1)}, u32[]{:S(2)}, u32[]{:S(2)}) collective-permute-start(bf16[1,264,1024]{2,1,0:T(8,128)(2,1)S(1)} %get-tuple-element.37), channel_id=1, source_target_pairs={{0,192},{8,200},{16,208},{24,216},{32,224},{40,232},{48,240},{56,2... | collective-permute-start | bytes 1622024 | tf_op jit(solution)/shard_map/ppermute | solution.py:361
  44.9 12.1 %collective-permute-start.14 = (bf16[2,128,128]{2,1,0:T(8,128)(2,1)S(1)}, bf16[2,128,128]{2,1,0:T(8,128)(2,1)S(1)}, u32[]{:S(2)}, u32[]{:S(2)}) collective-permute-start(bf16[2,128,128]{2,1,0:T(8,128)(2,1)S(1)} %get-tuple-element.43), channel_id=1, source_target_pairs={{0,128},{8,136},{16,144},{24,152},{32,160},{40,168},{48,176},{56,1... | collective-permute-start | bytes 196616 | tf_op jit(solution)/shard_map/ppermute | solution.py:361
  46.2 10.9 %collective-permute-start.15 = (bf16[2,128,128]{2,1,0:T(8,128)(2,1)S(1)}, bf16[2,128,128]{2,1,0:T(8,128)(2,1)S(1)}, u32[]{:S(2)}, u32[]{:S(2)}) collective-permute-start(bf16[2,128,128]{2,1,0:T(8,128)(2,1)S(1)} %get-tuple-element.44), channel_id=1, source_target_pairs={{0,168},{8,176},{16,184},{24,128},{32,136},{40,144},{48,152},{56,1... | collective-permute-start | bytes 196616 | tf_op jit(solution)/shard_map/ppermute | solution.py:361
  52.0 9.5 %collective-permute-start.16 = (bf16[2,128,128]{2,1,0:T(8,128)(2,1)S(1)}, bf16[2,128,128]{2,1,0:T(8,128)(2,1)S(1)}, u32[]{:S(2)}, u32[]{:S(2)}) collective-permute-start(bf16[2,128,128]{2,1,0:T(8,128)(2,1)S(1)} %get-tuple-element.45), channel_id=1, source_target_pairs={{0,152},{8,160},{16,168},{24,176},{32,184},{40,128},{48,136},{56,1... | collective-permute-start | bytes 196616 | tf_op jit(solution)/shard_map/ppermute | solution.py:361
